TPU v7x, 32 devices: a whole 2x2x4 slice. The times are simulated.
32 devices in a mesh: rad: 16 (over z, y, x), col: 2 (over core).
Axes of the slice: x: 2, y: 2, z: 4, core: 2. Of those that a mesh axis runs over, the one named last changes fastest.
Arguments:
- right_sides: bfloat16 [64, 384, 1024], P('rad', None, 'col'), may hold values from -6 to 6
- coarse_solution: bfloat16 [16, 384, 1024], P('rad', None, 'col'), may hold values from -6 to 6
- lift_one: bfloat16 [32, 2, 1024, 1024], P('rad', None, 'col'), may hold values from -0.125 to 0.125
- solve_one: bfloat16 [32, 3, 1024, 1024], P('rad', None, 'col'), may hold values from -0.109375 to 0.109375
- lift_two: bfloat16 [16, 2, 1024, 1024], P('rad', None, 'col'), may hold values from -0.125 to 0.125
- solve_two: bfloat16 [16, 3, 1024, 1024], P('rad', None, 'col'), may hold values from -0.109375 to 0.109375
Outputs:
- solution: bfloat16 [64, 384, 1024], P('rad', None, 'col')
- reduced_sides: bfloat16 [16, 384, 1024], P('rad', None, 'col')
All inputs are finite; a program needn't handle non-finite values.
Results may differ from a plain program's by a relative error of at most 0.007.
Values may be sent and summed in bfloat16 or wider, within the bound.
A program may use at most 64 MiB of HBM per device.

v0:
```python
import jax
import jax.numpy as jnp
from jax import lax
from jax.sharding import PartitionSpec as P


def padded(array, sides, width):
    for axis, dim in sides:
        peers, length = (lax.axis_size(axis), array.shape[dim])
        up = [(i, (i + 1) % peers) for i in range(peers - 1)]
        down = [(j, i) for i, j in up]
        last = lax.slice_in_dim(array, length - width, length, axis=dim)
        initial = lax.slice_in_dim(array, 0, width, axis=dim)
        before = lax.ppermute(last, axis, up)
        after = lax.ppermute(initial, axis, down)
        array = jnp.concatenate([before, array, after], axis=dim)
    return array


def passed_along(array, axis, by):
    peers = lax.axis_size(axis)
    pairs = [(i, i + by) for i in range(peers) if 0 <= i + by < peers]
    return lax.ppermute(array, axis, pairs)


def apply(vector, matrix):
    return lax.dot_general(
        vector, matrix, (((1,), (1,)), ((), ())), preferred_element_type=jnp.float32
    )


def local(right_sides, coarse_solution, lift_one, solve_one, lift_two, solve_two):
    coarse_here = coarse_solution[0]
    edge_blocks = jnp.stack([coarse_here, right_sides[1], right_sides[3]])
    haloed_local = padded(edge_blocks, (("rad", 0),), 1)
    haloed = lax.all_gather(haloed_local, "col", axis=2, tiled=True)
    before_odd = haloed[0]
    coarse_full = haloed[1]
    second_full = haloed[2]
    fourth_full = haloed[3]
    coarse_next = haloed[4]
    kept = (
        right_sides[0].astype(jnp.float32)
        - apply(before_odd, lift_one[0, 0])
        - apply(second_full, lift_one[0, 1])
    )
    kept = kept.astype(jnp.bfloat16)
    middle = (
        right_sides[2].astype(jnp.float32)
        - apply(second_full, lift_one[1, 0])
        - apply(fourth_full, lift_one[1, 1])
    )
    middle = middle.astype(jnp.bfloat16)
    middle_shifted = passed_along(middle, "rad", 1)
    middle_pair = lax.all_gather(jnp.stack([middle, middle_shifted]), "col", axis=2, tiled=True)
    middle_full = middle_pair[0]
    middle_before = middle_pair[1]
    reduced = (
        kept.astype(jnp.float32)
        - apply(middle_before, lift_two[0, 0])
        - apply(middle_full, lift_two[0, 1])
    )
    centre = (
        apply(middle_full, solve_two[0, 0])
        - apply(coarse_full, solve_two[0, 1])
        - apply(coarse_next, solve_two[0, 2])
    )
    centre = centre.astype(jnp.bfloat16)
    centre_full = lax.all_gather(centre, "col", axis=1, tiled=True)
    second = (
        apply(second_full, solve_one[0, 0])
        - apply(coarse_full, solve_one[0, 1])
        - apply(centre_full, solve_one[0, 2])
    )
    fourth = (
        apply(fourth_full, solve_one[1, 0])
        - apply(centre_full, solve_one[1, 1])
        - apply(coarse_next, solve_one[1, 2])
    )
    solved = jnp.stack(
        [coarse_here, second.astype(jnp.bfloat16), centre, fourth.astype(jnp.bfloat16)]
    )
    return (solved, reduced.astype(jnp.bfloat16)[None])


def solution(mesh):
    return jax.shard_map(
        local,
        mesh=mesh,
        in_specs=(
            P("rad", None, "col"),
            P("rad", None, "col"),
            P("rad", None, "col", None),
            P("rad", None, "col", None),
            P("rad", None, "col", None),
            P("rad", None, "col", None),
        ),
        out_specs=(P("rad", None, "col"), P("rad", None, "col")),
        check_vma=False,
    )
```

profile of v0, /device:TPU:13, one launch (start us, length us, event | category | flops | bytes accessed | tf_op | source)
XLA Modules:
  0.0 100.0 jit_solution(5105738647005974134)
XLA Ops:
  7.2 0.0 copy-start.2
  7.2 0.0 all-gather.3.cloned.1.call-start
  7.2 1.1 %slice.78 = bf16[1,384,512]{2,1,0:T(8,128)(2,1)S(1)} slice(bf16[4,384,512]{2,1,0:T(8,128)(2,1)} %param.6), slice={[3:4], [0:384], [0:512]} | slice | bytes 786432 | tf_op jit(solution)/shard_map/slice | solution.py:34
  8.4 3.1 %collective-permute-start = (bf16[1,384,512]{2,1,0:T(8,128)(2,1)S(1)}, bf16[1,384,512]{2,1,0:T(8,128)(2,1)S(1)}, u32[]{:S(2)}, u32[]{:S(2)}) collective-permute-start(bf16[1,384,512]{2,1,0:T(8,128)(2,1)S(1)} %slice.78), channel_id=1, source_target_pairs={{0,2},{2,4},{4,6},{6,8},{8,10},{10,12},{12,14},{14,16},{16,18},{18... | collective-permute-start | bytes 1179656 | tf_op jit(solution)/shard_map/ppermute | solution.py:14
  11.5 3.1 %collective-permute-start.1 = (bf16[1,384,512]{2,1,0:T(8,128)(2,1)}, bf16[1,384,512]{2,1,0:T(8,128)(2,1)S(1)}, u32[]{:S(2)}, u32[]{:S(2)}) collective-permute-start(bf16[1,384,512]{2,1,0:T(8,128)(2,1)} %param.7), channel_id=1, source_target_pairs={{2,0},{4,2},{6,4},{8,6},{10,8},{12,10},{14,12},{16,14},{18,16},{20... | collective-permute-start | bytes 1179656 | tf_op jit(solution)/shard_map/ppermute | solution.py:15
  14.6 6.6 %collective-permute-done = bf16[1,384,512]{2,1,0:T(8,128)(2,1)S(1)} collective-permute-done((bf16[1,384,512]{2,1,0:T(8,128)(2,1)S(1)}, bf16[1,384,512]{2,1,0:T(8,128)(2,1)S(1)}, u32[]{:S(2)}, u32[]{:S(2)}) %collective-permute-start) | collective-permute-done | bytes 393248 | tf_op jit(solution)/shard_map/ppermute | solution.py:14
  21.2 1.0 %constant_dynamic-update-slice_fusion.2 = bf16[5,384,512]{2,1,0:T(8,128)(2,1)S(1)} fusion(bf16[5,384,512]{2,1,0:T(8,128)(2,1)S(1)} %constant_dynamic-update-slice_fusion.3, bf16[1,384,512]{2,1,0:T(8,128)(2,1)} %param.7), kind=kLoop, calls=%fused_computation.67 | loop fusion | bytes 786432
  22.2 1.0 %slice_dynamic-update-slice_fusion = bf16[5,384,512]{2,1,0:T(8,128)(2,1)S(1)} fusion(bf16[5,384,512]{2,1,0:T(8,128)(2,1)S(1)} %constant_dynamic-update-slice_fusion.2, bf16[4,384,512]{2,1,0:T(8,128)(2,1)} %param.6), kind=kLoop, calls=%fused_computation.64 | loop fusion | bytes 786432
  23.2 0.0 copy-done.2
  23.3 7.3 %collective-permute-done.1 = bf16[1,384,512]{2,1,0:T(8,128)(2,1)S(1)} collective-permute-done((bf16[1,384,512]{2,1,0:T(8,128)(2,1)}, bf16[1,384,512]{2,1,0:T(8,128)(2,1)S(1)}, u32[]{:S(2)}, u32[]{:S(2)}) %collective-permute-start.1) | collective-permute-done | bytes 393248 | tf_op jit(solution)/shard_map/ppermute | solution.py:15
  30.6 0.0 copy-start
  30.6 1.3 %copy-done = bf16[5,384,512]{2,1,0:T(8,128)(2,1)} copy-done((bf16[5,384,512]{2,1,0:T(8,128)(2,1)}, bf16[5,384,512]{2,1,0:T(8,128)(2,1)S(1)}, u32[]{:S(2)}) %copy-start) | copy-done | bytes 1966104
  31.9 0.0 all-gather.3.cloned.1.call-update
  31.9 0.0 all-gather.5.cloned.1.call-start
  32.0 14.4 %all-gather.3.cloned.1.call-done = bf16[5,384,1024]{2,1,0:T(8,128)(2,1)} async-done(((bf16[5,384,512]{2,1,0:T(8,128)(2,1)}), bf16[5,384,1024]{2,1,0:T(8,128)(2,1)}) %all-gather.3.cloned.1.call-update) | async-done | bytes 3932176 | tf_op jit(solution)/shard_map/all_gather | solution.py:36
  46.3 2.1 %convolution_subtract_fusion.10 = f32[384,512]{1,0:T(8,128)S(1)} fusion(bf16[2,2,512,1024]{3,2,1,0:T(8,128)(2,1)} %param.8, bf16[5,384,1024]{2,1,0:T(8,128)(2,1)} %all-gather.3.cloned.1.call-done, bf16[4,384,512]{2,1,0:T(8,128)(2,1)S(1)} %copy-done.2), kind=kOutput, calls=%fused_computation.11 | convolution fusion | flops 403046400 | bytes 3014656 | tf_op jit(solution)/shard_map/dot_general | solution.py:27
  48.4 2.1 %fusion = bf16[384,512]{1,0:T(8,128)(2,1)S(1)} fusion(f32[384,512]{1,0:T(8,128)S(1)} %convolution_subtract_fusion.10, bf16[2,2,512,1024]{3,2,1,0:T(8,128)(2,1)} %param.8, bf16[5,384,1024]{2,1,0:T(8,128)(2,1)} %all-gather.3.cloned.1.call-done), kind=kOutput, calls=%fused_computation.13 | convolution fusion | flops 403046400 | bytes 3014656 | tf_op jit(solution)/shard_map/dot_general | solution.py:27
  50.5 3.1 %collective-permute-start.2 = (bf16[384,512]{1,0:T(8,128)(2,1)S(1)}, bf16[384,512]{1,0:T(8,128)(2,1)S(1)}, u32[]{:S(2)}, u32[]{:S(2)}) collective-permute-start(bf16[384,512]{1,0:T(8,128)(2,1)S(1)} %fusion), channel_id=1, source_target_pairs={{0,2},{2,4},{4,6},{6,8},{8,10},{10,12},{12,14},{14,16},{16,18},{18... | collective-permute-start | bytes 1179656 | tf_op jit(solution)/shard_map/ppermute | solution.py:23
  53.6 10.2 %collective-permute-done.2 = bf16[384,512]{1,0:T(8,128)(2,1)S(1)} collective-permute-done((bf16[384,512]{1,0:T(8,128)(2,1)S(1)}, bf16[384,512]{1,0:T(8,128)(2,1)S(1)}, u32[]{:S(2)}, u32[]{:S(2)}) %collective-permute-start.2) | collective-permute-done | bytes 393248 | tf_op jit(solution)/shard_map/ppermute | solution.py:23
  63.8 0.9 pad_maximum_fusion.1
  64.7 0.0 all-gather.5.cloned.1.call-update
  64.8 2.1 %fusion.25 = f32[384,512]{1,0:T(8,128)S(1)} fusion(bf16[2,3,512,1024]{3,2,1,0:T(8,128)(2,1)} %param.9, bf16[5,384,1024]{2,1,0:T(8,128)(2,1)} %all-gather.3.cloned.1.call-done), kind=kOutput, calls=%fused_computation.38 | convolution fusion | flops 402653184 | bytes 2621440 | tf_op jit(solution)/shard_map/dot_general | solution.py:27
  66.8 2.1 %convolution_subtract_fusion.3 = f32[384,512]{1,0:T(8,128)S(1)} fusion(bf16[2,2,512,1024]{3,2,1,0:T(8,128)(2,1)} %param.8, bf16[5,384,1024]{2,1,0:T(8,128)(2,1)} %all-gather.3.cloned.1.call-done, bf16[4,384,512]{2,1,0:T(8,128)(2,1)S(1)} %copy-done.2), kind=kOutput, calls=%fused_computation.4 | convolution fusion | flops 403046400 | bytes 3014656 | tf_op jit(solution)/shard_map/dot_general | solution.py:27
  68.9 2.1 %fusion.5 = f32[384,512]{1,0:T(8,128)S(1)} fusion(f32[384,512]{1,0:T(8,128)S(1)} %convolution_subtract_fusion.3, bf16[2,2,512,1024]{3,2,1,0:T(8,128)(2,1)} %param.8, bf16[5,384,1024]{2,1,0:T(8,128)(2,1)} %all-gather.3.cloned.1.call-done), kind=kOutput, calls=%fused_computation.18 | convolution fusion | flops 403243008 | bytes 3407872 | tf_op jit(solution)/shard_map/dot_general | solution.py:27
  71.0 2.2 %convolution_subtract_fusion.11 = f32[384,512]{1,0:T(8,128)S(1)} fusion(f32[384,512]{1,0:T(8,128)S(1)} %fusion.25, bf16[2,3,512,1024]{3,2,1,0:T(8,128)(2,1)} %param.9, bf16[5,384,1024]{2,1,0:T(8,128)(2,1)} %all-gather.3.cloned.1.call-done), kind=kOutput, calls=%fused_computation.12 | convolution fusion | flops 402849792 | bytes 3407872 | tf_op jit(solution)/shard_map/dot_general | solution.py:27
  73.2 2.6 %all-gather.5.cloned.1.call-done = bf16[2,384,1024]{2,1,0:T(8,128)(2,1)} async-done(((bf16[2,384,512]{2,1,0:T(8,128)(2,1)}), bf16[2,384,1024]{2,1,0:T(8,128)(2,1)}) %all-gather.5.cloned.1.call-update) | async-done | bytes 1572880 | tf_op jit(solution)/shard_map/all_gather | solution.py:55
  75.8 0.0 slice-start
  75.8 2.2 %fusion.21 = f32[384,512]{1,0:T(8,128)S(1)} fusion(bf16[1,3,512,1024]{3,2,1,0:T(8,128)(2,1)} %param.11, bf16[2,384,1024]{2,1,0:T(8,128)(2,1)} %all-gather.5.cloned.1.call-done), kind=kOutput, calls=%fused_computation.34 | convolution fusion | flops 402653184 | bytes 2621440 | tf_op jit(solution)/shard_map/dot_general | solution.py:27
  78.0 0.0 slice-start.1
  78.0 2.2 %convolution_subtract_fusion.8 = f32[384,512]{1,0:T(8,128)S(1)} fusion(f32[384,512]{1,0:T(8,128)S(1)} %fusion.21, bf16[1,3,512,1024]{3,2,1,0:T(8,128)(2,1)} %param.11, bf16[5,384,1024]{2,1,0:T(8,128)(2,1)} %all-gather.3.cloned.1.call-done), kind=kOutput, calls=%fused_computation.9 | convolution fusion | flops 402849792 | bytes 3407872 | tf_op jit(solution)/shard_map/dot_general | solution.py:27
  80.3 2.1 %fusion.1 = bf16[384,512]{1,0:T(8,128)(2,1)S(1)} fusion(f32[384,512]{1,0:T(8,128)S(1)} %convolution_subtract_fusion.8, bf16[1,3,512,1024]{3,2,1,0:T(8,128)(2,1)} %param.11, bf16[5,384,1024]{2,1,0:T(8,128)(2,1)} %all-gather.3.cloned.1.call-done), kind=kOutput, calls=%fused_computation.14 | convolution fusion | flops 403046400 | bytes 3014656 | tf_op jit(solution)/shard_map/dot_general | solution.py:27
  82.3 2.4 %all_gather.11 = bf16[384,1024]{1,0:T(8,128)(2,1)S(1)} all-gather(bf16[384,512]{1,0:T(8,128)(2,1)S(1)} %fusion.1), channel_id=1, replica_groups=mesh['rad'=16,'col'=2] {'col'}, dimensions={1}, use_global_device_ids=true | all-gather | bytes 1179648 | tf_op jit(solution)/shard_map/all_gather | solution.py:69
  84.7 0.0 slice-done
  84.7 0.0 slice-done.1
  84.7 0.6 fusion.15
  85.4 0.7 fusion.9
  86.0 0.0 copy-start.1
  86.1 1.8 %convolution_subtract_fusion.5 = f32[384,512]{1,0:T(8,128)S(1)} fusion(f32[384,512]{1,0:T(8,128)S(1)} %fusion.15, bf16[2,3,512,1024]{3,2,1,0:T(8,128)(2,1)S(1)} %bitcast.93, bf16[5,384,1024]{2,1,0:T(8,128)(2,1)} %all-gather.3.cloned.1.call-done), kind=kOutput, calls=%fused_computation.6 | convolution fusion | flops 402849792 | bytes 3407872 | tf_op jit(solution)/shard_map/dot_general | solution.py:27
  87.9 0.0 copy-start.3
  87.9 0.0 copy-start.4
  87.9 1.9 %fusion.8 = bf16[1,384,512]{2,1,0:T(8,128)(2,1)S(1)} fusion(f32[384,512]{1,0:T(8,128)S(1)} %convolution_subtract_fusion.5, bf16[2,3,512,1024]{3,2,1,0:T(8,128)(2,1)S(1)} %bitcast.93, bf16[5,384,1024]{2,1,0:T(8,128)(2,1)} %all-gather.3.cloned.1.call-done), kind=kOutput, calls=%fused_computation.21 | convolution fusion | flops 403046400 | bytes 3014656 | tf_op jit(solution)/shard_map/dot_general | solution.py:27
  89.9 0.0 copy-done.1
  89.9 1.3 %pad_maximum_fusion = bf16[4,384,512]{2,1,0:T(8,128)(2,1)} fusion(bf16[1,384,512]{2,1,0:T(8,128)(2,1)S(1)} %fusion.8, bf16[1,384,512]{2,1,0:T(8,128)(2,1)S(1)} %bitcast.89, bf16[1,384,512]{2,1,0:T(8,128)(2,1)S(1)} %fusion.9, bf16[1,384,512]{2,1,0:T(8,128)(2,1)S(1)} %copy-done.1), kind=kLoop, calls=%fused_computation | loop fusion | flops 2359296 | bytes 3145728 | tf_op jit(solution)/shard_map/stack | solution.py:80
  91.2 0.0 copy-done.3
  91.2 0.0 copy-done.4
  91.2 0.6 convolution_subtract_fusion.1
  91.8 1.4 %fusion.7 = bf16[1,384,512]{2,1,0:T(8,128)(2,1)} fusion(f32[384,512]{1,0:T(8,128)S(1)} %convolution_subtract_fusion.1, bf16[1,2,512,1024]{3,2,1,0:T(8,128)(2,1)S(1)} %copy-done.3, bf16[2,384,1024]{2,1,0:T(8,128)(2,1)S(1)} %copy-done.4), kind=kOutput, calls=%fused_computation.20 | convolution fusion | flops 403046400 | bytes 3014656 | tf_op jit(solution)/shard_map/dot_general | solution.py:27
  (4 shorter events, 0.1 us)
Async XLA Ops:
  7.2 16.1 %copy-start.2 = (bf16[4,384,512]{2,1,0:T(8,128)(2,1)S(1)}, bf16[4,384,512]{2,1,0:T(8,128)(2,1)}, u32[]{:S(2)}) copy-start(bf16[4,384,512]{2,1,0:T(8,128)(2,1)} %param.6) | copy-start | bytes 4718596
  7.2 39.2 %all-gather.3.cloned.1.call-start = ((), (), s32[]{:S(2)}) async-start(), calls=%async_computation | async-start | bytes 5898240 | tf_op jit(solution)/shard_map/all_gather | solution.py:36
  8.4 12.8 %collective-permute-start = (bf16[1,384,512]{2,1,0:T(8,128)(2,1)S(1)}, bf16[1,384,512]{2,1,0:T(8,128)(2,1)S(1)}, u32[]{:S(2)}, u32[]{:S(2)}) collective-permute-start(bf16[1,384,512]{2,1,0:T(8,128)(2,1)S(1)} %slice.78), channel_id=1, source_target_pairs={{0,2},{2,4},{4,6},{6,8},{8,10},{10,12},{12,14},{14,16},{16,18},{18... | collective-permute-start | bytes 1179656 | tf_op jit(solution)/shard_map/ppermute | solution.py:14
  11.5 19.1 %collective-permute-start.1 = (bf16[1,384,512]{2,1,0:T(8,128)(2,1)}, bf16[1,384,512]{2,1,0:T(8,128)(2,1)S(1)}, u32[]{:S(2)}, u32[]{:S(2)}) collective-permute-start(bf16[1,384,512]{2,1,0:T(8,128)(2,1)} %param.7), channel_id=1, source_target_pairs={{2,0},{4,2},{6,4},{8,6},{10,8},{12,10},{14,12},{16,14},{18,16},{20... | collective-permute-start | bytes 1179656 | tf_op jit(solution)/shard_map/ppermute | solution.py:15
  30.6 1.3 %copy-start = (bf16[5,384,512]{2,1,0:T(8,128)(2,1)}, bf16[5,384,512]{2,1,0:T(8,128)(2,1)S(1)}, u32[]{:S(2)}) copy-start(bf16[5,384,512]{2,1,0:T(8,128)(2,1)S(1)} %constant_dynamic-update-slice_fusion) | copy-start | bytes 5898244
  31.9 43.9 %all-gather.5.cloned.1.call-start = ((), (), s32[]{:S(2)}) async-start(), calls=%async_computation.1 | async-start | bytes 2359296 | tf_op jit(solution)/shard_map/all_gather | solution.py:55
  50.5 13.3 %collective-permute-start.2 = (bf16[384,512]{1,0:T(8,128)(2,1)S(1)}, bf16[384,512]{1,0:T(8,128)(2,1)S(1)}, u32[]{:S(2)}, u32[]{:S(2)}) collective-permute-start(bf16[384,512]{1,0:T(8,128)(2,1)S(1)} %fusion), channel_id=1, source_target_pairs={{0,2},{2,4},{4,6},{6,8},{8,10},{10,12},{12,14},{14,16},{16,18},{18... | collective-permute-start | bytes 1179656 | tf_op jit(solution)/shard_map/ppermute | solution.py:23
  75.8 8.9 %slice-start = ((s8[6291456]{0:T(1024)(128)(4,1)}), s8[4194304]{0:T(1024)(128)(4,1)S(1)}, s32[]{:S(2)}) async-start(s8[6291456]{0:T(1024)(128)(4,1)} %bitcast.92), calls=%async_computation.2 | async-start | bytes 8388608
  78.0 6.7 %slice-start.1 = ((s8[6291456]{0:T(1024)(128)(4,1)}), s8[2097152]{0:T(1024)(128)(4,1)S(1)}, s32[]{:S(2)}) async-start(s8[6291456]{0:T(1024)(128)(4,1)} %bitcast.92), calls=%async_computation.3 | async-start | bytes 4194304
  86.0 3.8 %copy-start.1 = (bf16[1,384,512]{2,1,0:T(8,128)(2,1)S(1)}, bf16[1,384,512]{2,1,0:T(8,128)(2,1)}, u32[]{:S(2)}) copy-start(bf16[1,384,512]{2,1,0:T(8,128)(2,1)} %param.7) | copy-start | bytes 1179652
  87.9 3.3 %copy-start.3 = (bf16[1,2,512,1024]{3,2,1,0:T(8,128)(2,1)S(1)}, bf16[1,2,512,1024]{3,2,1,0:T(8,128)(2,1)}, u32[]{:S(2)}) copy-start(bf16[1,2,512,1024]{3,2,1,0:T(8,128)(2,1)} %param.10) | copy-start | bytes 6291460
  87.9 3.3 %copy-start.4 = (bf16[2,384,1024]{2,1,0:T(8,128)(2,1)S(1)}, bf16[2,384,1024]{2,1,0:T(8,128)(2,1)}, u32[]{:S(2)}) copy-start(bf16[2,384,1024]{2,1,0:T(8,128)(2,1)} %all-gather.5.cloned.1.call-done) | copy-start | bytes 4718596
Sparse Core Ops, SparseCore 0:
  32.0 14.2 all-gather.2
  64.9 10.8 all-gather.4
where the time goes:
time: 101 us; the launch traced here: 100 us
  waiting for transfers between devices  41.1 us (41%)
  matrix products  26.1 us (26%)
  between operations  14.3 us (14%)
  starting transfers between devices  9.36 us (9%)
  local copies, waits for them, and re-layouts  4.58 us (5%)
  blocking collectives  2.37 us (2%)
  other arithmetic  2.29 us (2%)
    dot_general x15, matrix products, apply(): lax.dot_general(vector, matrix, (((1,), (1,)), ((), ())), preferred_eleme...  26.1 us
    all_gather x1, waiting for transfers between devices, local(): haloed = lax.all_gather(haloed_local, 'col', axis=2, tiled=True)  14.4 us
    ppermute x1, waiting for transfers between devices, passed_along(): return lax.ppermute(array, axis, pairs)  10.2 us
    ppermute x1, waiting for transfers between devices, padded(): after = lax.ppermute(initial, axis, down)  7.29 us
    ppermute x1, waiting for transfers between devices, padded(): before = lax.ppermute(last, axis, up)  6.58 us
    unnamed x18, local copies, waits for them, and re-layouts  3.42 us
    ppermute x1, starting transfers between devices, padded(): before = lax.ppermute(last, axis, up)  3.12 us
    ppermute x1, starting transfers between devices, passed_along(): return lax.ppermute(array, axis, pairs)  3.1 us
  transfers between devices with their start and end apart: 5, of which 5 were waited for; matrix products, arithmetic and copies ran while one was open for 11% of the time, Pallas kernels for 0%

commit v1 on v0

v1 whole, which is shorter than its diff:
```python
import functools

import jax
import jax.numpy as jnp
from jax import lax
from jax.experimental import pallas as pl
from jax.experimental.pallas import tpu as pltpu
from jax.sharding import PartitionSpec as P

MESH = pl.DeviceIdType.MESH
F32 = jnp.float32
BF16 = jnp.bfloat16

B1, B3, COARSE, BEFORE, NEXT, MID, MIDBEF, CENTRE = range(8)
KEPT, RED, CEN, SEC, FOU = range(5)
L1, S1, L2, S2 = range(4)
WEIGHTS = (
    (L1, 1, 0), (L1, 1, 1), (L1, 0, 1), (S1, 0, 0), (S1, 1, 0), (S1, 0, 1), (S2, 0, 1), (S2, 0, 0),
    (L2, 0, 1), (S2, 0, 2), (S1, 1, 2), (S1, 0, 2), (S1, 1, 1), (L1, 0, 0), (L2, 0, 0),
)
SLOT = {w: i for i, w in enumerate(WEIGHTS)}


def kernel(R, C, NQ, rs, co, l1, s1, l2, s2, sol, red,
           full, wv, own, acc, stage, wsem, lsem, osem, csend, crecv, rsend, rrecv):
    V, D = rs.shape[1], rs.shape[2]
    Q = V // NQ
    TN = min(256, D)
    r = lax.axis_index("rad")
    c = lax.axis_index("col")
    has_up, has_down = r < R - 1, r > 0
    mats = (l1, s1, l2, s2)

    def load(i):
        m, a, b = WEIGHTS[i]
        return pltpu.make_async_copy(mats[m].at[a, b], wv.at[i], wsem.at[i])

    locals_ = (
        pltpu.make_async_copy(rs.at[1], full.at[B1, c], lsem.at[0]),
        pltpu.make_async_copy(rs.at[3], full.at[B3, c], lsem.at[1]),
        pltpu.make_async_copy(co.at[0], full.at[COARSE, c], lsem.at[2]),
        pltpu.make_async_copy(rs.at[2], own.at[1], lsem.at[3]),
        pltpu.make_async_copy(rs.at[0], own.at[0], lsem.at[4]),
    )
    keep = pltpu.make_async_copy(co.at[0], sol.at[0], osem.at[0])

    def across(tag, slot, rows, src):
        out = []
        for d in range(1, C):
            peer = lax.rem(c + d, C)
            out.append(pltpu.make_async_remote_copy(
                src_ref=src,
                dst_ref=full.at[tag, c, rows],
                send_sem=csend.at[slot, d - 1],
                recv_sem=crecv.at[slot, d - 1],
                device_id={"col": peer},
                device_id_type=MESH,
            ))
        return out

    def arrived(tag, slot, rows):
        for d in range(1, C):
            peer = lax.rem(c + C - d, C)
            pltpu.make_async_remote_copy(
                src_ref=full.at[tag, peer, rows],
                dst_ref=full.at[tag, peer, rows],
                send_sem=csend.at[slot, d - 1],
                recv_sem=crecv.at[slot, d - 1],
                device_id={"col": peer},
                device_id_type=MESH,
            ).wait_recv()

    every = pl.ds(0, V)

    def part(q):
        return pl.ds(q * Q, Q)

    def along(kind, q):
        tag = (NEXT, BEFORE, MIDBEF)[kind]
        src = (co.at[0, part(q)], rs.at[3, part(q)], full.at[MID, c, part(q)])[kind]
        return pltpu.make_async_remote_copy(
            src_ref=src,
            dst_ref=full.at[tag, c, part(q)],
            send_sem=rsend.at[kind, q],
            recv_sem=rrecv.at[kind, q],
            device_id={"rad": r - 1 if kind == 0 else r + 1},
            device_id_type=MESH,
        )

    def slot_of(tag, q=0):
        if tag in (B1, B3, COARSE, MID, CENTRE):
            return (B1, B3, COARSE, MID, CENTRE).index(tag)
        return 5 + (NEXT, BEFORE, MIDBEF).index(tag) * NQ + q

    locals_[0].start()
    locals_[1].start()
    load(0).start()
    load(1).start()
    locals_[3].start()

    barrier = pltpu.get_barrier_semaphore()
    for d in range(1, C):
        pl.semaphore_signal(barrier, inc=1, device_id={"col": lax.rem(c + d, C)}, device_id_type=MESH)

    @pl.when(has_up)
    def _():
        pl.semaphore_signal(barrier, inc=1, device_id={"rad": r + 1}, device_id_type=MESH)

    @pl.when(has_down)
    def _():
        pl.semaphore_signal(barrier, inc=1, device_id={"rad": r - 1}, device_id_type=MESH)

    pl.semaphore_wait(barrier, C - 1 + has_up.astype(jnp.int32) + has_down.astype(jnp.int32))

    sent = []

    def share(tag, slot, rows, src):
        for copy in across(tag, slot, rows, src):
            copy.start()
            sent.append(copy)

    @pl.when(has_down)
    def _():
        for q in range(NQ):
            along(0, q).start()

    share(B1, slot_of(B1), every, rs.at[1])
    share(B3, slot_of(B3), every, rs.at[3])

    @pl.when(has_up)
    def _():
        for q in range(NQ):
            along(1, q).start()

    share(COARSE, slot_of(COARSE), every, co.at[0])
    locals_[2].start()
    locals_[4].start()
    for i in range(2, len(WEIGHTS)):
        load(i).start()
    keep.start()

    @pl.when(r == 0)
    def _():
        full[BEFORE] = jnp.zeros_like(full[BEFORE])
        full[MIDBEF] = jnp.zeros_like(full[MIDBEF])

    @pl.when(r == R - 1)
    def _():
        full[NEXT] = jnp.zeros_like(full[NEXT])

    def times(tag, weight, rows, columns):
        i = SLOT[weight]
        total = None
        for s in range(C):
            term = lax.dot_general(
                full[tag, s, rows, :], wv[i, columns, s * D:(s + 1) * D],
                (((1,), (1,)), ((), ())), preferred_element_type=F32,
            )
            total = term if total is None else total + term
        return total

    def tiles(body):
        @pl.loop(0, D // TN)
        def _(t):
            body(pl.ds(pl.multiple_of(t * TN, TN), TN))

    def ready(*weights):
        for w in weights:
            load(SLOT[w]).wait()

    locals_[0].wait()
    locals_[1].wait()
    locals_[3].wait()
    ready((L1, 1, 0), (L1, 1, 1))
    arrived(B1, slot_of(B1), every)
    arrived(B3, slot_of(B3), every)

    def mid(n):
        full[MID, c, :, n] = (
            own[1, :, n].astype(F32) - times(B1, (L1, 1, 0), every, n) - times(B3, (L1, 1, 1), every, n)
        ).astype(BF16)

    tiles(mid)
    share(MID, slot_of(MID), every, full.at[MID, c])

    @pl.when(has_up)
    def _():
        for q in range(NQ):
            along(2, q).start()

    locals_[4].wait()
    ready((L1, 0, 1), (S1, 0, 0), (S1, 1, 0))

    def first(n):
        acc[KEPT, :, n] = own[0, :, n].astype(F32) - times(B1, (L1, 0, 1), every, n)
        acc[FOU, :, n] = times(B3, (S1, 1, 0), every, n)

    tiles(first)
    locals_[2].wait()
    arrived(COARSE, slot_of(COARSE), every)
    ready((S1, 0, 1), (S2, 0, 1))

    def with_coarse(n):
        acc[SEC, :, n] = times(B1, (S1, 0, 0), every, n) - times(COARSE, (S1, 0, 1), every, n)

    tiles(with_coarse)
    arrived(MID, slot_of(MID), every)
    ready((S2, 0, 0), (L2, 0, 1))

    def with_mid(n):
        acc[CEN, :, n] = times(MID, (S2, 0, 0), every, n) - times(COARSE, (S2, 0, 1), every, n)
        acc[RED, :, n] = times(MID, (L2, 0, 1), every, n)

    tiles(with_mid)

    def relay(kind, tag, there, q):
        @pl.when(there)
        def _():
            along(kind, q).wait_recv()
            for copy in across(tag, slot_of(tag, q), part(q), full.at[tag, c, part(q)]):
                copy.start()

    def relayed(tag, there, q):
        @pl.when(there)
        def _():
            arrived(tag, slot_of(tag, q), part(q))

    for q in range(NQ):
        relay(0, NEXT, has_up, q)
    ready((S2, 0, 2), (S1, 1, 2))
    for q in range(NQ):
        relayed(NEXT, has_up, q)

    def centre(n):
        full[CENTRE, c, :, n] = (acc[CEN, :, n] - times(NEXT, (S2, 0, 2), every, n)).astype(BF16)

    tiles(centre)
    share(CENTRE, slot_of(CENTRE), every, full.at[CENTRE, c])
    centre_out = pltpu.make_async_copy(full.at[CENTRE, c], sol.at[2], osem.at[1])
    centre_out.start()

    def with_next(n):
        acc[FOU, :, n] = acc[FOU, :, n] - times(NEXT, (S1, 1, 2), every, n)

    tiles(with_next)
    ready((S1, 0, 2), (S1, 1, 1))
    arrived(CENTRE, slot_of(CENTRE), every)

    def odd(n):
        stage[0, :, n] = (acc[SEC, :, n] - times(CENTRE, (S1, 0, 2), every, n)).astype(BF16)
        stage[1, :, n] = (acc[FOU, :, n] - times(CENTRE, (S1, 1, 1), every, n)).astype(BF16)

    tiles(odd)
    second_out = pltpu.make_async_copy(stage.at[0], sol.at[1], osem.at[2])
    fourth_out = pltpu.make_async_copy(stage.at[1], sol.at[3], osem.at[3])
    second_out.start()
    fourth_out.start()

    for q in range(NQ):
        relay(1, BEFORE, has_down, q)
    ready((L1, 0, 0))
    for q in range(NQ):
        relayed(BEFORE, has_down, q)

    def kept(n):
        whole = (acc[KEPT, :, n] - times(BEFORE, (L1, 0, 0), every, n)).astype(BF16)
        acc[RED, :, n] = whole.astype(F32) - acc[RED, :, n]

    tiles(kept)

    ready((L2, 0, 0))
    reds = [pltpu.make_async_copy(stage.at[2, part(q)], red.at[0, part(q)], osem.at[4 + q]) for q in range(NQ)]

    def last(q):
        relayed(MIDBEF, has_down, q)

        def body(n):
            stage[2, part(q), n] = (
                acc[RED, part(q), n] - times(MIDBEF, (L2, 0, 0), part(q), n)
            ).astype(BF16)

        tiles(body)
        reds[q].start()

    for q in range(NQ):
        relay(2, MIDBEF, has_down, q)
        if q > 0:
            last(q - 1)
    last(NQ - 1)

    for copy in sent:
        copy.wait_send()

    @pl.when(has_down)
    def _():
        for q in range(NQ):
            along(0, q).wait_send()
            for tag in (BEFORE, MIDBEF):
                for copy in across(tag, slot_of(tag, q), part(q), full.at[tag, c, part(q)]):
                    copy.wait_send()

    @pl.when(has_up)
    def _():
        for q in range(NQ):
            along(1, q).wait_send()
            along(2, q).wait_send()
            for copy in across(NEXT, slot_of(NEXT, q), part(q), full.at[NEXT, c, part(q)]):
                copy.wait_send()

    keep.wait()
    centre_out.wait()
    second_out.wait()
    fourth_out.wait()
    for copy in reds:
        copy.wait()


def local(R, C, right_sides, coarse_solution, lift_one, solve_one, lift_two, solve_two):
    _, V, D = right_sides.shape
    K = lift_one.shape[-1]
    NQ = 4 if V % 64 == 0 else 1
    peers = max(C - 1, 1)
    moved = sum(a.size for a in (right_sides, coarse_solution, lift_one, solve_one, lift_two, solve_two))
    any_ = pl.BlockSpec(memory_space=pl.ANY)
    return pl.pallas_call(
        functools.partial(kernel, R, C, NQ),
        out_shape=(
            jax.ShapeDtypeStruct(right_sides.shape, BF16),
            jax.ShapeDtypeStruct(coarse_solution.shape, BF16),
        ),
        in_specs=[any_] * 6,
        out_specs=(any_, any_),
        scratch_shapes=[
            pltpu.VMEM((8, C, V, D), BF16),
            pltpu.VMEM((len(WEIGHTS), D, K), BF16),
            pltpu.VMEM((2, V, D), BF16),
            pltpu.VMEM((5, V, D), F32),
            pltpu.VMEM((3, V, D), BF16),
            pltpu.SemaphoreType.DMA((len(WEIGHTS),)),
            pltpu.SemaphoreType.DMA((5,)),
            pltpu.SemaphoreType.DMA((4 + NQ,)),
            pltpu.SemaphoreType.DMA((5 + 3 * NQ, peers)),
            pltpu.SemaphoreType.DMA((5 + 3 * NQ, peers)),
            pltpu.SemaphoreType.DMA((3, NQ)),
            pltpu.SemaphoreType.DMA((3, NQ)),
        ],
        compiler_params=pltpu.CompilerParams(
            collective_id=0, has_side_effects=True, vmem_limit_bytes=48 * 1024 * 1024
        ),
        cost_estimate=pl.CostEstimate(
            flops=2 * len(WEIGHTS) * V * D * K, bytes_accessed=4 * moved, transcendentals=0
        ),
    )(right_sides, coarse_solution, lift_one, solve_one, lift_two, solve_two)


def solution(mesh):
    return jax.shard_map(
        functools.partial(local, mesh.shape["rad"], mesh.shape["col"]),
        mesh=mesh,
        in_specs=(
            P("rad", None, "col"),
            P("rad", None, "col"),
            P("rad", None, "col", None),
            P("rad", None, "col", None),
            P("rad", None, "col", None),
            P("rad", None, "col", None),
        ),
        out_specs=(P("rad", None, "col"), P("rad", None, "col")),
        check_vma=False,
    )
```

time: 101 us -> 48.7 us (0.48)
  Pallas kernels: 0 us -> 41.9 us
  waiting for transfers between devices: 41.1 us -> 0 us
  matrix products: 26.1 us -> 0 us
  between operations: 14.3 us -> 0.65 us
  starting transfers between devices: 9.36 us -> 0 us
  blocking collectives: 2.37 us -> 0 us
  other arithmetic: 2.29 us -> 0 us
  local copies, waits for them, and re-layouts: 4.58 us -> 5.88 us
    pallas_call x0 -> x1, Pallas kernels: none -> 41.9 us  [local(): pl.pallas_call(functools.partial(kernel, R, C, NQ), out_shape=(jax.ShapeD...]
    dot_general x15 -> x0, matrix products: 26.1 us -> none  [apply(): lax.dot_general(vector, matrix, (((1,), (1,)), ((), ())), preferred_eleme...]
    ppermute x3 -> x0, waiting for transfers between devices: 24.1 us -> none  [the longest x1 10.2 us: passed_along(): return lax.ppermute(array, axis, pairs)]
    all_gather x2 -> x0, waiting for transfers between devices: 17 us -> none  [the longest x1 14.4 us: local(): haloed = lax.all_gather(haloed_local, 'col', axis=2, tiled=True)]
    ppermute x3 -> x0, starting transfers between devices: 9.28 us -> none  [the longest x1 3.12 us: padded(): before = lax.ppermute(last, axis, up)]
    unnamed x18 -> x8, local copies, waits for them, and re-layouts: 3.42 us -> 5.88 us
    all_gather x1 -> x0, blocking collectives: 2.37 us -> none  [local(): centre_full = lax.all_gather(centre, 'col', axis=1, tiled=True)]
    another operation x2 -> x0, other arithmetic: 2.29 us -> none  [the longest x1 1.34 us: local(): jnp.stack([coarse_here, second.astype(jnp.bfloat16), centre, fourth.astyp...]
  transfers between devices with their start and end apart: 5 -> 0, of which waited for: 5 -> 0; matrix products, arithmetic and copies ran while one was open for 11% -> 0% of each run, Pallas kernels for 0% -> 0%
where the time goes in v1:
time: 48.7 us; the launch traced here: 48.5 us
  Pallas kernels  41.9 us (86%)
  local copies, waits for them, and re-layouts  5.88 us (12%)
  between operations  0.65 us (1%)
    pallas_call x1, Pallas kernels, local(): pl.pallas_call(functools.partial(kernel, R, C, NQ), out_shape=(jax.ShapeD...  41.9 us
    unnamed x8, local copies, waits for them, and re-layouts  5.88 us

profile of v1, /device:TPU:13, one launch (start us, length us, event | category | flops | bytes accessed | tf_op | source)
XLA Modules:
  0.0 48.5 jit_solution(4265210770506110738)
XLA Ops:
  0.6 0.0 copy-start
  0.6 1.6 %copy-done = bf16[1,2,512,1024]{3,2,1,0:T(8,128)(2,1)S(1)} copy-done((bf16[1,2,512,1024]{3,2,1,0:T(8,128)(2,1)S(1)}, bf16[1,2,512,1024]{3,2,1,0:T(8,128)(2,1)}, u32[]{:S(2)}) %copy-start) | copy-done | bytes 2097176
  2.2 0.0 copy-start.1
  2.2 1.4 %copy-done.1 = bf16[4,384,512]{2,1,0:T(8,128)(2,1)S(1)} copy-done((bf16[4,384,512]{2,1,0:T(8,128)(2,1)S(1)}, bf16[4,384,512]{2,1,0:T(8,128)(2,1)}, u32[]{:S(2)}) %copy-start.1) | copy-done | bytes 1572888
  3.6 0.0 copy-start.2
  3.6 1.0 %copy-done.2 = bf16[1,384,512]{2,1,0:T(8,128)(2,1)S(1)} copy-done((bf16[1,384,512]{2,1,0:T(8,128)(2,1)S(1)}, bf16[1,384,512]{2,1,0:T(8,128)(2,1)}, u32[]{:S(2)}) %copy-start.2) | copy-done | bytes 393240
  4.6 41.9 %shard_map.77 = (bf16[4,384,512]{2,1,0:T(8,128)(2,1)S(1)}, bf16[1,384,512]{2,1,0:T(8,128)(2,1)S(1)}) custom-call(bf16[4,384,512]{2,1,0:T(8,128)(2,1)S(1)} %copy-done.1, bf16[1,384,512]{2,1,0:T(8,128)(2,1)S(1)} %copy-done.2, bf16[2,2,512,1024]{3,2,1,0:T(8,128)(2,1)} %l1.1, bf16[2,3,512,1024]{3,2,1,0:T(8,128)(2,1)} %s1_.1, ...), custom_call_target="tpu_custom_call" | custom-call | flops 6039797760 | bytes 35389440 | tf_op jit(solution)/shard_map/pallas_call | solution.py:325
  46.6 1.1 %copy.10 = bf16[4,384,512]{2,1,0:T(8,128)(2,1)} copy(bf16[4,384,512]{2,1,0:T(8,128)(2,1)S(1)} %get-tuple-element.4) | data formatting | bytes 3145728
  47.7 0.7 %copy.11 = bf16[1,384,512]{2,1,0:T(8,128)(2,1)} copy(bf16[1,384,512]{2,1,0:T(8,128)(2,1)S(1)} %get-tuple-element.5) | data formatting | bytes 786432
Async XLA Ops:
  0.6 1.6 %copy-start = (bf16[1,2,512,1024]{3,2,1,0:T(8,128)(2,1)S(1)}, bf16[1,2,512,1024]{3,2,1,0:T(8,128)(2,1)}, u32[]{:S(2)}) copy-start(bf16[1,2,512,1024]{3,2,1,0:T(8,128)(2,1)} %l2.1) | copy-start | bytes 6291460
  2.2 1.4 %copy-start.1 = (bf16[4,384,512]{2,1,0:T(8,128)(2,1)S(1)}, bf16[4,384,512]{2,1,0:T(8,128)(2,1)}, u32[]{:S(2)}) copy-start(bf16[4,384,512]{2,1,0:T(8,128)(2,1)} %rs.1) | copy-start | bytes 4718596
  3.6 1.0 %copy-start.2 = (bf16[1,384,512]{2,1,0:T(8,128)(2,1)S(1)}, bf16[1,384,512]{2,1,0:T(8,128)(2,1)}, u32[]{:S(2)}) copy-start(bf16[1,384,512]{2,1,0:T(8,128)(2,1)} %co.1) | copy-start | bytes 1179652

commit v2 on v1

--- a/solution.py
+++ b/solution.py
@@ -127,11 +127,6 @@
     share(B1, slot_of(B1), every, rs.at[1])
     share(B3, slot_of(B3), every, rs.at[3])
 
-    @pl.when(has_up)
-    def _():
-        for q in range(NQ):
-            along(1, q).start()
-
     share(COARSE, slot_of(COARSE), every, co.at[0])
     locals_[2].start()
     locals_[4].start()
@@ -183,11 +178,6 @@
     tiles(mid)
     share(MID, slot_of(MID), every, full.at[MID, c])
 
-    @pl.when(has_up)
-    def _():
-        for q in range(NQ):
-            along(2, q).start()
-
     locals_[4].wait()
     ready((L1, 0, 1), (S1, 0, 0), (S1, 1, 0))
 
@@ -212,6 +202,7 @@
         acc[RED, :, n] = times(MID, (L2, 0, 1), every, n)
 
     tiles(with_mid)
+
 
     def relay(kind, tag, there, q):
         @pl.when(there)
@@ -227,6 +218,18 @@
 
     for q in range(NQ):
         relay(0, NEXT, has_up, q)
+    @pl.when(has_down)
+    def _():
+        for q in range(NQ):
+            along(0, q).wait_send()
+
+    @pl.when(has_up)
+    def _():
+        for q in range(NQ):
+            along(1, q).start()
+        for q in range(NQ):
+            along(2, q).start()
+
     ready((S2, 0, 2), (S1, 1, 2))
     for q in range(NQ):
         relayed(NEXT, has_up, q)
@@ -256,6 +259,7 @@
     second_out.start()
     fourth_out.start()
 
+
     for q in range(NQ):
         relay(1, BEFORE, has_down, q)
     ready((L1, 0, 0))
@@ -294,7 +298,6 @@
     @pl.when(has_down)
     def _():
         for q in range(NQ):
-            along(0, q).wait_send()
             for tag in (BEFORE, MIDBEF):
                 for copy in across(tag, slot_of(tag, q), part(q), full.at[tag, c, part(q)]):
                     copy.wait_send()
@@ -328,7 +331,7 @@
             jax.ShapeDtypeStruct(right_sides.shape, BF16),
             jax.ShapeDtypeStruct(coarse_solution.shape, BF16),
         ),
-        in_specs=[any_] * 6,
+        in_specs=[pl.BlockSpec(memory_space=pltpu.HBM)] * 6,
         out_specs=(any_, any_),
         scratch_shapes=[
             pltpu.VMEM((8, C, V, D), BF16),
@@ -345,7 +348,7 @@
             pltpu.SemaphoreType.DMA((3, NQ)),
         ],
         compiler_params=pltpu.CompilerParams(
-            collective_id=0, has_side_effects=True, vmem_limit_bytes=48 * 1024 * 1024
+            collective_id=0, has_side_effects=True, vmem_limit_bytes=60 * 1024 * 1024
         ),
         cost_estimate=pl.CostEstimate(
             flops=2 * len(WEIGHTS) * V * D * K, bytes_accessed=4 * moved, transcendentals=0

time: 48.7 us -> 39.8 us (0.82)
  the two profiles are of different devices: /device:TPU:13 before, /device:TPU:17 now
where the time goes in v2:
time: 39.8 us; the launch traced here: 39.7 us
  Pallas kernels  35.6 us (89%)
  local copies, waits for them, and re-layouts  3.45 us (9%)
  between operations  0.65 us (2%)
    pallas_call x1, Pallas kernels, local(): pl.pallas_call(functools.partial(kernel, R, C, NQ), out_shape=(jax.ShapeD...  35.6 us
    unnamed x4, local copies, waits for them, and re-layouts  3.45 us

profile of v2, /device:TPU:17, one launch (start us, length us, event | category | flops | bytes accessed | tf_op | source)
XLA Modules:
  0.0 39.7 jit_solution(13312947718298651074)
XLA Ops:
  0.6 35.6 %shard_map.77 = (bf16[4,384,512]{2,1,0:T(8,128)(2,1)}, bf16[1,384,512]{2,1,0:T(8,128)(2,1)}) custom-call(bf16[4,384,512]{2,1,0:T(8,128)(2,1)} %rs.1, bf16[1,384,512]{2,1,0:T(8,128)(2,1)} %co.1, bf16[2,2,512,1024]{3,2,1,0:T(8,128)(2,1)} %l1.1, bf16[2,3,512,1024]{3,2,1,0:T(8,128)(2,1)} %s1_.1, bf16[1,2,512,1024]{3,2,1,0:T(8,128)(2,1)} %l2.1, ...), custom_call_target="tpu_custom_call" | custom-call | flops 6039797760 | bytes 35389440 | tf_op jit(solution)/shard_map/pallas_call | solution.py:328
  36.2 0.0 copy-start
  36.2 2.7 %copy.10 = bf16[4,384,512]{2,1,0:T(8,128)(2,1)} copy(bf16[4,384,512]{2,1,0:T(8,128)(2,1)} %get-tuple-element.4) | data formatting | bytes 3145728
  38.9 0.0 copy-done
  38.9 0.7 %copy.11 = bf16[1,384,512]{2,1,0:T(8,128)(2,1)} copy(bf16[1,384,512]{2,1,0:T(8,128)(2,1)S(1)} %copy-done) | data formatting | bytes 786432
Async XLA Ops:
  36.2 2.7 %copy-start = (bf16[1,384,512]{2,1,0:T(8,128)(2,1)S(1)}, bf16[1,384,512]{2,1,0:T(8,128)(2,1)}, u32[]{:S(2)}) copy-start(bf16[1,384,512]{2,1,0:T(8,128)(2,1)} %get-tuple-element.5) | copy-start | bytes 1179652
